TPU v7x, 256 devices: a whole 4x4x8 slice. The times are simulated.
256 devices in a mesh: dp: 8 (over y, x_lo), shard: 32 (over x_hi, z, core).
Axes of the slice: x: 4 (x_hi: 2, x_lo: 2; x = x_hi * 2 + x_lo), y: 4, z: 8, core: 2. Of those that a mesh axis runs over, the one named last changes fastest.
Arguments:
- grad_parts: bfloat16 [8, 96, 512, 2048], P('dp', None, 'shard'), may hold values from -40 to 40
- momentum: float32 [96, 512, 2048], P('dp', 'shard'), may hold values from -8 to 8
- weight: bfloat16 [96, 512, 2048], P('dp', 'shard'), may hold values from -4 to 4
Outputs:
- new_momentum: float32 [96, 512, 2048], P('dp', 'shard')
- update: float32 [96, 512, 2048], P('dp', 'shard')
- new_weight: bfloat16 [96, 512, 2048], P('dp', 'shard')
All inputs are finite; a program needn't handle non-finite values.
Results may differ from a plain program's by a relative error of at most 0.02.
Values may be sent and summed in bfloat16 or wider, within the bound.
A program may use at most 128 MiB of HBM per device.

v0:
```python
import math

import jax
import jax.numpy as jnp
from jax import lax
from jax.sharding import PartitionSpec as P

ROWS = 512
COLS = 2048
ITERS = 5


linear_term = 3.4445
square_term = -4.775
fourth_term = 2.0315
decay_rate = 0.95
step_size = 0.05
tiny_norm = 1e-07


def newton_schulz(start):
    current = start
    for step in range(ITERS):
        gram = lax.dot_general(
            current, current, (((1,), (1,)), ((), ())), preferred_element_type=jnp.float32
        )
        square = jnp.dot(
            gram, gram, preferred_element_type=jnp.float32, precision=lax.Precision.HIGHEST
        )
        poly = (square_term * gram + fourth_term * square).astype(jnp.bfloat16)
        current = (
            linear_term * current.astype(jnp.float32)
            + jnp.dot(poly, current, preferred_element_type=jnp.float32)
        ).astype(jnp.bfloat16)
    return current


def body(grad_parts, momentum, weight):
    group = momentum.shape[0]
    shard_rows = momentum.shape[1]
    columns = momentum.shape[2]
    shards = lax.axis_size("shard")
    whole_rows = shard_rows * shards
    gradient = lax.psum_scatter(
        grad_parts.astype(jnp.float32), "dp", scatter_dimension=1, tiled=True
    )[0]
    next_moment = decay_rate * momentum + gradient
    nesterov = gradient + decay_rate * next_moment
    owners = jnp.arange(group, dtype=jnp.int32) * shards // group
    selector = owners[None, :] == jnp.arange(shards, dtype=jnp.int32)[:, None]
    my_index = lax.axis_index("shard")
    is_owner = jnp.any(owners == my_index)
    slots = jnp.einsum(
        "sk,krc->src", selector.astype(jnp.float32), nesterov, precision=lax.Precision.HIGHEST
    )
    received = lax.all_to_all(slots, "shard", split_axis=0, concat_axis=0, tiled=True).reshape(
        whole_rows, columns
    )
    total = jnp.sum(received * received)
    start = (received / (jnp.sqrt(total) + tiny_norm)).astype(jnp.bfloat16)
    result = lax.cond(is_owner, newton_schulz, jnp.zeros_like, start)
    returned = lax.all_to_all(
        result.reshape(shards, shard_rows, columns),
        "shard",
        split_axis=0,
        concat_axis=0,
        tiled=True,
    )
    mine = jnp.einsum(
        "sk,src->krc", selector.astype(jnp.bfloat16), returned, preferred_element_type=jnp.float32
    )
    shape_scale = 0.2 * math.sqrt(max(ROWS, COLS))
    scaled = shape_scale * mine
    fresh = (weight.astype(jnp.float32) - step_size * scaled).astype(jnp.bfloat16)
    return (next_moment, scaled, fresh)


def solution(mesh):
    return jax.shard_map(
        body,
        mesh=mesh,
        in_specs=(P("dp", None, "shard", None), P("dp", "shard", None), P("dp", "shard", None)),
        out_specs=(P("dp", "shard", None), P("dp", "shard", None), P("dp", "shard", None)),
        check_vma=False,
    )
```

profile of v0, /device:TPU:1, one launch (start us, length us, event | category | flops | bytes accessed | tf_op | source)
XLA Modules:
  0.0 489.7 jit_solution(12375094210027526051)
XLA Ops:
  7.2 0.0 reduce-scatter.2.cloned.1.call-start
  7.2 8.9 %convert_element_type.68 = f32[1,96,16,2048]{3,2,1,0:T(8,128)} convert(bf16[1,96,16,2048]{3,2,1,0:T(8,128)(2,1)} %param.5) | non-fusion elementwise | flops 3145728 | bytes 18874368 | tf_op jit(solution)/shard_map/convert_element_type | solution.py:45
  16.1 0.0 copy-start.1
  16.1 0.0 reduce-scatter.2.cloned.1.call-update
  16.1 254.6 %reduce-scatter.2.cloned.1.call-done = f32[1,12,16,2048]{3,2,1,0:T(8,128)} async-done(((f32[1,96,16,2048]{3,2,1,0:T(8,128)}), f32[1,12,16,2048]{3,2,1,0:T(8,128)}) %reduce-scatter.2.cloned.1.call-update) | async-done | bytes 1572880 | tf_op jit(solution)/shard_map/reduce_scatter | solution.py:44
  270.7 0.0 copy-done.1
  270.7 2.9 bitcast_add_fusion
  273.6 2.6 fusion.12
  276.2 4.4 copy.18
  280.6 10.0 %all-to-all-start = ((f32[32,16,2048]{2,1,0:T(8,128)}), f32[32,16,2048]{2,1,0:T(8,128)}, u32[]{:S(2)}, u32[]{:S(2)}) async-start(f32[32,16,2048]{2,1,0:T(8,128)} %copy.18), calls=%async_computation.1 | async-start | bytes 8388608 | tf_op jit(solution)/shard_map/all_to_all | solution.py:56
  290.6 0.6 compare_reduce_fusion
  291.9 94.9 %all-to-all-done = f32[32,16,2048]{2,1,0:T(8,128)} async-done(((f32[32,16,2048]{2,1,0:T(8,128)}), f32[32,16,2048]{2,1,0:T(8,128)}, u32[]{:S(2)}, u32[]{:S(2)}) %all-to-all-start) | async-done | bytes 4194336 | tf_op jit(solution)/shard_map/all_to_all | solution.py:56
  386.7 3.9 multiply_reduce_fusion
  391.3 4.0 divide_convert_fusion
  395.3 0.5 conditional.1
  395.3 0.2 broadcast.44
  395.8 0.0 copy-start.2
  395.8 80.4 %all_to_all.10 = bf16[32,16,2048]{2,1,0:T(8,128)(2,1)S(1)} all-to-all(bf16[32,16,2048]{2,1,0:T(8,128)(2,1)S(1)} %bitcast.42), channel_id=1, replica_groups=mesh['dp'=8,'shard'=32] {'shard'}, dimensions={0} | all-to-all | bytes 4194304 | tf_op jit(solution)/shard_map/all_to_all | solution.py:62
  476.2 0.0 copy-done.2
  476.2 3.3 subtract_convert_fusion
  479.5 2.1 copy.21
  481.5 1.3 copy.22
  (1 shorter events, 0.0 us)
Async XLA Ops:
  7.2 263.6 %reduce-scatter.2.cloned.1.call-start = ((), (), s32[]{:S(2)}) async-start(), calls=%async_computation.3 | async-start | bytes 14155776 | tf_op jit(solution)/shard_map/reduce_scatter | solution.py:44
  16.1 254.7 %copy-start.1 = (f32[12,16,2048]{2,1,0:T(8,128)S(1)}, f32[12,16,2048]{2,1,0:T(8,128)}, u32[]{:S(2)}) copy-start(f32[12,16,2048]{2,1,0:T(8,128)} %param.6) | copy-start | bytes 4718596
  280.6 106.1 %all-to-all-start = ((f32[32,16,2048]{2,1,0:T(8,128)}), f32[32,16,2048]{2,1,0:T(8,128)}, u32[]{:S(2)}, u32[]{:S(2)}) async-start(f32[32,16,2048]{2,1,0:T(8,128)} %copy.18), calls=%async_computation.1 | async-start | bytes 8388608 | tf_op jit(solution)/shard_map/all_to_all | solution.py:56
  395.8 80.4 %copy-start.2 = (bf16[12,16,2048]{2,1,0:T(8,128)(2,1)S(1)}, bf16[12,16,2048]{2,1,0:T(8,128)(2,1)}, u32[]{:S(2)}) copy-start(bf16[12,16,2048]{2,1,0:T(8,128)(2,1)} %param.7) | copy-start | bytes 2359300
Sparse Core Ops, SparseCore 0:
  16.2 254.4 reduce-scatter.1
where the time goes:
time: 491 us; the launch traced here: 490 us
  waiting for transfers between devices  349 us (71%)
  blocking collectives  80.4 us (16%)
  other arithmetic  20.2 us (4%)
  between operations  15.4 us (3%)
  starting transfers between devices  10 us (2%)
  local copies, waits for them, and re-layouts  8.02 us (2%)
  matrix products  5.88 us (1%)
    reduce_scatter x1, waiting for transfers between devices, body(): lax.psum_scatter(grad_parts.astype(jnp.float32), 'dp', scatter_dimension=...  255 us
    all_to_all x1, waiting for transfers between devices, body(): lax.all_to_all(slots, 'shard', split_axis=0, concat_axis=0, tiled=True)  94.9 us
    all_to_all x1, blocking collectives, body(): lax.all_to_all(result.reshape(shards, shard_rows, columns), 'shard', spli...  80.4 us
    all_to_all x1, starting transfers between devices, body(): lax.all_to_all(slots, 'shard', split_axis=0, concat_axis=0, tiled=True)  9.98 us
  transfers between devices with their start and end apart: 2, of which 2 were waited for; matrix products, arithmetic and copies ran while one was open for 0% of the time, Pallas kernels for 0%

commit v1 on v0

v1 whole, which is shorter than its diff:
```python
import functools
import math

import jax
import jax.numpy as jnp
from jax import lax
from jax.experimental import pallas as pl
from jax.experimental.pallas import tpu as pltpu
from jax.sharding import PartitionSpec as P

MESH = pl.DeviceIdType.MESH
F32 = jnp.float32
BF16 = jnp.bfloat16

MATS = 12
ROWS = 512
COLS = 2048
BAND = 16
SHARDS = 32
ITERS = 5
NA = 8
NB = MATS - NA
HB = NB // 2

CHUNKS = 8
WIDTH = COLS // CHUNKS
AHEAD = 2

linear_term = 3.4445
square_term = -4.775
fourth_term = 2.0315
decay_rate = 0.95
step_size = 0.05
tiny_norm = 1e-07

A_R, A_D, A_S, A_X, B_X, B_R, B_D, B_S = 0, 2, 4, 6, 7, 8, 10, 12
KINDS = 14


def owner_of(k):
    return 2 * ((4 * k) // 3)


def dot(a, b):
    return jnp.dot(a, b, preferred_element_type=F32)


def dot_t(a, b):
    return lax.dot_general(a, b, (((1,), (1,)), ((), ())), preferred_element_type=F32)


def poly_of(gram_ref, poly_ref, scale2):
    half = ROWS // 2
    top = gram_ref[:half, :] * scale2
    low = gram_ref[half:, half:] * scale2
    high_top = top.astype(BF16)
    rest_top = (top - high_top.astype(F32)).astype(BF16)
    high_low = low.astype(BF16)
    rest_low = (low - high_low.astype(F32)).astype(BF16)
    corner = top[:, half:].T
    high_corner = corner.astype(BF16)
    rest_corner = (corner - high_corner.astype(F32)).astype(BF16)
    high_bottom = jnp.concatenate([high_corner, high_low], axis=1)
    rest_bottom = jnp.concatenate([rest_corner, rest_low], axis=1)
    high = jnp.concatenate([high_top, high_bottom], axis=0)
    rest = jnp.concatenate([rest_top, rest_bottom], axis=0)
    cross_top = dot(high_top, rest)
    cross_bottom = dot(high_bottom, rest)
    square_top = dot(high_top, high)
    square_low = dot(high_bottom, high[:, half:])
    flipped = jnp.concatenate([cross_top[:, :half].T, cross_bottom[:, :half].T], axis=1)
    poly_top = square_term * top + fourth_term * (square_top + (cross_top + flipped))
    cross_low = cross_bottom[:, half:]
    poly_low = square_term * low + fourth_term * (square_low + (cross_low + cross_low.T))
    poly_ref[:half, :] = poly_top.astype(BF16)
    poly_ref[half:, half:] = poly_low.astype(BF16)
    poly_ref[half:, :half] = poly_top[:, half:].T.astype(BF16)


def add_gram(gram_ref, block):
    half = ROWS // 2
    gram_ref[:half, :] += dot_t(block[:half], block)
    gram_ref[half:, half:] += dot_t(block[half:], block[half:])


def clear_gram(gram_ref):
    gram_ref[...] = jnp.zeros_like(gram_ref)


NSW = 512


def orthogonalize(source, work, gram_ref, poly_ref, send):
    half = ROWS // 2
    row = lax.broadcasted_iota(jnp.int32, (half, half), 0)
    col = lax.broadcasted_iota(jnp.int32, (half, half), 1)
    diag = jnp.where(row == col, gram_ref[:half, :half] + gram_ref[half:, half:], 0.0)
    total = jnp.sum(jnp.sum(diag, axis=1, keepdims=True), axis=0, keepdims=True)
    scale = 1.0 / (jnp.sqrt(total) + tiny_norm)

    def apply(src, c, factor):
        cols = pl.ds(pl.multiple_of(c * NSW, NSW), NSW)
        block = src[:, :, cols].reshape(ROWS, NSW)
        new = linear_term * block.astype(F32) + dot(poly_ref[...], block)
        if factor is not None:
            new = new * factor
        new = new.astype(BF16)
        work[:, :, cols] = new.reshape(SHARDS, BAND, NSW)
        return new

    poly_of(gram_ref, poly_ref, scale * scale)
    clear_gram(gram_ref)

    @pl.loop(0, COLS // NSW)
    def _(c):
        add_gram(gram_ref, apply(source, c, scale))

    @pl.loop(0, ITERS - 2)
    def _(it):
        poly_of(gram_ref, poly_ref, 1.0)
        clear_gram(gram_ref)

        @pl.loop(0, COLS // NSW)
        def _(c):
            add_gram(gram_ref, apply(work, c, None))

    poly_of(gram_ref, poly_ref, 1.0)

    @pl.loop(0, COLS // NSW)
    def _(c):
        apply(work, c, None)
        send(c)


def kernel(
    grads, momentum, moment_out, ortho_out,
    own_p, own_m, own_c, own_b, a_r, a_d, a_s, a_x, a_send, ax_send,
    b_x, b_u, b_r, b_d, b_s, b_send,
    nest, gathered, work, gram_ref, poly_ref,
    load_sem, send_sem, recv_sem, gsend_sem, grecv_sem, ssend_sem, srecv_sem,
):
    dp = lax.axis_index("dp")
    me = lax.axis_index("shard")
    y, x = dp // 2, dp % 2
    other = 1 - x
    up_y, down_y, far_y = (y + 1) % 4, (y + 3) % 4, (y + 2) % 4
    up = (up_y * 2 + x, me)
    down = (down_y * 2 + x, me)
    partner = (y * 2 + other, me)
    way = (up, down)

    loads = [
        pltpu.make_async_copy(grads.at[up_y, 0, pl.ds(0, NA)], own_p, load_sem.at[0]),
        pltpu.make_async_copy(grads.at[down_y, 1, pl.ds(0, NA)], own_m, load_sem.at[1]),
        pltpu.make_async_copy(grads.at[y, :, pl.ds(0, NA)], own_c, load_sem.at[2]),
        pltpu.make_async_copy(grads.at[:, x, pl.ds(NA, NB)], own_b, load_sem.at[3]),
    ]
    for load in loads:
        load.start()

    barrier = pltpu.get_barrier_semaphore()
    for device in (up, down, partner):
        pl.semaphore_signal(barrier, inc=1, device_id=device, device_id_type=MESH)

    @pl.loop(1, SHARDS)
    def _(r):
        pl.semaphore_signal(barrier, inc=1, device_id=(dp, (me + r) % SHARDS), device_id_type=MESH)

    pl.semaphore_wait(barrier, 3 + SHARDS - 1)

    for load in loads:
        load.wait()

    def columns(c):
        return pl.ds(pl.multiple_of(c * WIDTH, WIDTH), WIDTH)

    def message(kind, c, src, dst, device):
        return pltpu.make_async_remote_copy(
            src_ref=src, dst_ref=dst, send_sem=send_sem.at[kind, c], recv_sem=recv_sem.at[kind, c],
            device_id=device, device_id_type=MESH,
        )

    def a_relay(g, c):
        cols = columns(c)
        return message(A_R + g, c, grads.at[far_y, g, pl.ds(0, NA), :, cols], a_r.at[g, :, :, cols], way[g])

    def a_direct(g, c):
        cols = columns(c)
        target = (down_y, up_y)[g]
        return message(A_D + g, c, grads.at[target, g, pl.ds(0, NA), :, cols], a_d.at[g, :, :, cols], way[1 - g])

    def a_sum(g, c):
        cols = columns(c)
        return message(A_S + g, c, a_send.at[g, :, :, cols], a_s.at[g, :, :, cols], way[g])

    def a_cross(c):
        cols = columns(c)
        return message(A_X, c, ax_send.at[:, :, cols], a_x.at[:, :, cols], partner)

    def b_cross(c):
        cols = columns(c)
        return message(B_X, c, grads.at[:, other, pl.ds(NA, NB), :, cols], b_x.at[:, :, :, cols], partner)

    def b_relay(g, c):
        cols = columns(c)
        return message(B_R + g, c, b_u.at[far_y, pl.ds(g * HB, HB), :, cols], b_r.at[g, :, :, cols], way[g])

    def b_direct(g, c):
        cols = columns(c)
        target = (down_y, up_y)[g]
        return message(B_D + g, c, b_u.at[target, pl.ds(g * HB, HB), :, cols], b_d.at[g, :, :, cols], way[1 - g])

    def b_sum(g, c):
        cols = columns(c)
        return message(B_S + g, c, b_send.at[g, :, :, cols], b_s.at[g, :, :, cols], way[g])

    def issue(c):
        b_cross(c).start()
        for g in (0, 1):
            a_relay(g, c).start()
        for g in (0, 1):
            a_direct(g, c).start()

    def stage1(c):
        cols = columns(c)
        own = (own_p, own_m)
        for g in (0, 1):
            a_relay(g, c).wait_recv()
            total = own[g][:, :, cols].astype(F32) + a_r[g, :, :, cols].astype(F32)
            a_send[g, :, :, cols] = total.astype(BF16)
            a_sum(g, c).start()
        b_cross(c).wait_recv()
        for t in range(4):
            total = own_b[t, :, :, cols].astype(F32) + b_x[t, :, :, cols].astype(F32)
            b_u[t, :, :, cols] = total.astype(BF16)
        for g in (0, 1):
            b_relay(g, c).start()
        for g in (0, 1):
            b_direct(g, c).start()

    def a_total(g, c):
        cols = columns(c)
        return own_c[g, :, :, cols].astype(F32) + a_d[g, :, :, cols].astype(F32) + a_s[g, :, :, cols].astype(F32)

    def stage2(c):
        cols = columns(c)
        for g in (0, 1):
            a_direct(g, c).wait_recv()
            a_sum(g, c).wait_recv()
        ax_send[:, :, cols] = a_total(other, c).astype(BF16)
        a_cross(c).start()
        own = (up_y, down_y)
        for g in (0, 1):
            b_relay(g, c).wait_recv()
            mine = own_b[own[g], g * HB:(g + 1) * HB, :, cols].astype(F32)
            crossed = b_x[own[g], g * HB:(g + 1) * HB, :, cols].astype(F32)
            b_send[g, :, :, cols] = (mine + crossed + b_r[g, :, :, cols].astype(F32)).astype(BF16)
            b_sum(g, c).start()

    def finish(first, gradient, cols):
        count = gradient.shape[0]
        moment = decay_rate * momentum[first:first + count, :, cols] + gradient
        moment_out[first:first + count, :, cols] = moment
        nest[first:first + count, :, cols] = (gradient + decay_rate * moment).astype(BF16)

    def to_owner(k, c):
        cols = columns(c)
        return pltpu.make_async_remote_copy(
            src_ref=nest.at[k, :, cols], dst_ref=gathered.at[me, :, cols],
            send_sem=gsend_sem.at[k], recv_sem=grecv_sem.at[c],
            device_id=(dp, owner_of(k)), device_id_type=MESH,
        )

    def stage3(c):
        cols = columns(c)
        for g in (0, 1):
            b_direct(g, c).wait_recv()
            b_sum(g, c).wait_recv()
            mine = own_b[y, g * HB:(g + 1) * HB, :, cols].astype(F32)
            crossed = b_x[y, g * HB:(g + 1) * HB, :, cols].astype(F32)
            arrived = b_d[g, :, :, cols].astype(F32) + b_s[g, :, :, cols].astype(F32)
            finish(NA + g * HB, mine + crossed + arrived, cols)
        a_cross(c).wait_recv()
        finish(0, a_total(x, c) + a_x[:, :, cols].astype(F32), cols)

        @pl.loop(0, MATS)
        def _(k):
            mine = owner_of(k) == me

            @pl.when(mine)
            def _():
                pltpu.make_async_copy(nest.at[k, :, cols], gathered.at[me, :, cols], grecv_sem.at[c]).start()

            @pl.when(jnp.logical_not(mine))
            def _():
                to_owner(k, c).start()

    for c in range(AHEAD):
        issue(c)

    def guarded(step, offset, stage):
        @pl.when(jnp.logical_and(step >= offset, step < CHUNKS + offset))
        def _():
            stage(step - offset)

    @pl.loop(0, CHUNKS + 2)
    def _(step):
        guarded(step, 0, stage1)
        guarded(step, 1, stage2)
        guarded(step, 2, stage3)
        guarded(step, -AHEAD, issue)

    chip = me // 2
    slot = (3 * chip + 3) // 4
    is_owner = jnp.logical_and(me % 2 == 0, chip % 4 != 3)

    @pl.when(is_owner)
    def _():
        clear_gram(gram_ref)

        @pl.loop(0, CHUNKS)
        def _(c):
            cols = columns(c)
            whole = gathered.at[:, :, cols]
            pltpu.make_async_copy(whole, whole, grecv_sem.at[c]).wait()
            add_gram(gram_ref, gathered[:, :, cols].reshape(ROWS, WIDTH))

        def scatter(c):
            cols = pl.ds(pl.multiple_of(c * NSW, NSW), NSW)
            pltpu.make_async_copy(work.at[me, :, cols], ortho_out.at[slot, :, cols], srecv_sem.at[slot]).start()

            @pl.loop(1, SHARDS)
            def _(r):
                to = (me + r) % SHARDS
                pltpu.make_async_remote_copy(
                    src_ref=work.at[to, :, cols], dst_ref=ortho_out.at[slot, :, cols],
                    send_sem=ssend_sem.at[c], recv_sem=srecv_sem.at[slot],
                    device_id=(dp, to), device_id_type=MESH,
                ).start()

        orthogonalize(gathered, work, gram_ref, poly_ref, scatter)

    @pl.loop(0, MATS)
    def _(k):
        whole = ortho_out.at[k]
        pltpu.make_async_copy(whole, whole, srecv_sem.at[k]).wait()

        @pl.when(owner_of(k) != me)
        def _():
            pltpu.make_async_copy(nest.at[k], nest.at[k], gsend_sem.at[k]).wait()

    @pl.loop(0, CHUNKS)
    def _(c):
        for g in (0, 1):
            a_relay(g, c).wait_send()
            a_direct(g, c).wait_send()
            a_sum(g, c).wait_send()
            b_relay(g, c).wait_send()
            b_direct(g, c).wait_send()
            b_sum(g, c).wait_send()
        a_cross(c).wait_send()
        b_cross(c).wait_send()

    @pl.when(is_owner)
    def _():
        @pl.loop(0, COLS // NSW)
        def _(c):
            sent = work.at[pl.ds(0, SHARDS - 1), :, pl.ds(pl.multiple_of(c * NSW, NSW), NSW)]
            pltpu.make_async_copy(sent, sent, ssend_sem.at[c]).wait()


def body(grad_parts, momentum, weight):
    vmem = pl.BlockSpec(memory_space=pltpu.VMEM)
    grads = grad_parts.reshape(4, 2, MATS, BAND, COLS)
    a_block, b_block = (NA, BAND, COLS), (HB, BAND, COLS)

    def buf(*shape):
        return pltpu.VMEM(shape, BF16)

    moment, ortho = pl.pallas_call(
        kernel,
        out_shape=(
            jax.ShapeDtypeStruct((MATS, BAND, COLS), F32),
            jax.ShapeDtypeStruct((MATS, BAND, COLS), BF16),
        ),
        in_specs=[pl.BlockSpec(memory_space=pl.ANY), vmem],
        out_specs=(vmem, vmem),
        scratch_shapes=[
            buf(*a_block), buf(*a_block), buf(2, *a_block), buf(4, NB, BAND, COLS),
            buf(2, *a_block), buf(2, *a_block), buf(2, *a_block), buf(*a_block), buf(2, *a_block), buf(*a_block),
            buf(4, NB, BAND, COLS), buf(4, NB, BAND, COLS),
            buf(2, *b_block), buf(2, *b_block), buf(2, *b_block), buf(2, *b_block),
            buf(MATS, BAND, COLS),
            buf(SHARDS, BAND, COLS), buf(SHARDS, BAND, COLS),
            pltpu.VMEM((ROWS, ROWS), F32), pltpu.VMEM((ROWS, ROWS), BF16),
            pltpu.SemaphoreType.DMA((4,)),
            pltpu.SemaphoreType.DMA((KINDS, CHUNKS)), pltpu.SemaphoreType.DMA((KINDS, CHUNKS)),
            pltpu.SemaphoreType.DMA((MATS,)), pltpu.SemaphoreType.DMA((CHUNKS,)),
            pltpu.SemaphoreType.DMA((COLS // NSW,)), pltpu.SemaphoreType.DMA((MATS,)),
        ],
        compiler_params=pltpu.CompilerParams(
            collective_id=0, has_side_effects=True, vmem_limit_bytes=56 * 1024 * 1024
        ),
        name="muon_step",
    )(grads, momentum)
    shape_scale = 0.2 * math.sqrt(max(ROWS, COLS))
    scaled = shape_scale * ortho.astype(F32)
    fresh = (weight.astype(F32) - step_size * scaled).astype(BF16)
    return (moment, scaled, fresh)


def solution(mesh):
    return jax.shard_map(
        body,
        mesh=mesh,
        in_specs=(P("dp", None, "shard", None), P("dp", "shard", None), P("dp", "shard", None)),
        out_specs=(P("dp", "shard", None), P("dp", "shard", None), P("dp", "shard", None)),
        check_vma=False,
    )
```

time: 491 us -> 120 us (0.24)
  waiting for transfers between devices: 349 us -> 0 us
  Pallas kernels: 0 us -> 115 us
  blocking collectives: 80.4 us -> 0 us
  other arithmetic: 20.2 us -> 2.99 us
  between operations: 15.4 us -> 0.66 us
  starting transfers between devices: 10 us -> 0 us
  local copies, waits for them, and re-layouts: 8.02 us -> 1.15 us
  matrix products: 5.88 us -> 0 us
    reduce_scatter x1 -> x0, waiting for transfers between devices: 255 us -> none  [body(): lax.psum_scatter(grad_parts.astype(jnp.float32), 'dp', scatter_dimension=...]
    pallas_call x0 -> x1, Pallas kernels: none -> 115 us  [body(): pl.pallas_call(kernel, out_shape=(jax.ShapeDtypeStruct((MATS, BAND, COLS)...]
    all_to_all x1 -> x0, waiting for transfers between devices: 94.9 us -> none  [body(): lax.all_to_all(slots, 'shard', split_axis=0, concat_axis=0, tiled=True)]
    all_to_all x1 -> x0, blocking collectives: 80.4 us -> none  [body(): lax.all_to_all(result.reshape(shards, shard_rows, columns), 'shard', spli...]
    all_to_all x1 -> x0, starting transfers between devices: 9.98 us -> none  [body(): lax.all_to_all(slots, 'shard', split_axis=0, concat_axis=0, tiled=True)]
    convert_element_type x2 -> x1, other arithmetic: 12.8 us -> 2.99 us  [body(): fresh = (weight.astype(F32) - step_size * scaled).astype(BF16)]
    dot_general x2 -> x0, matrix products: 5.88 us -> none  [the longest x1 3.3 us: body(): jnp.einsum('sk,src->krc', selector.astype(jnp.bfloat16), returned, prefer...]
  transfers between devices with their start and end apart: 2 -> 0, of which waited for: 2 -> 0; matrix products, arithmetic and copies ran while one was open for 0% -> 0% of each run, Pallas kernels for 0% -> 0%
where the time goes in v1:
time: 120 us
  Pallas kernels  115 us (96%)
  other arithmetic  2.99 us (2%)
    pallas_call x1, Pallas kernels, body(): pl.pallas_call(kernel, out_shape=(jax.ShapeDtypeStruct((MATS, BAND, COLS)...  115 us
    convert_element_type x1, other arithmetic, body(): fresh = (weight.astype(F32) - step_size * scaled).astype(BF16)  2.99 us

profile of v1, /device:TPU:1, one launch (start us, length us, event | category | flops | bytes accessed | tf_op | source)
XLA Modules:
  0.0 120.1 jit_solution(4193622370671993792)
XLA Ops:
  0.6 0.0 copy-start.1
  0.6 115.3 %muon_step.1 = (f32[12,16,2048]{2,1,0:T(8,128)}, bf16[12,16,2048]{2,1,0:T(8,128)(2,1)}) custom-call(bf16[4,2,12,16,2048]{4,3,2,1,0:T(8,128)(2,1)} %bitcast.1, f32[12,16,2048]{2,1,0:T(8,128)} %momentum.1), custom_call_target="tpu_custom_call" | custom-call | tf_op jit(solution)/shard_map/muon_step/pallas_call | solution.py:380
  115.9 0.0 copy-done.1
  115.9 0.0 copy-start
  115.9 3.0 %fusion.1 = (bf16[12,16,2048]{2,1,0:T(8,128)(2,1)}, f32[12,16,2048]{2,1,0:T(8,128)}) fusion(bf16[12,16,2048]{2,1,0:T(8,128)(2,1)} %get-tuple-element.6, bf16[12,16,2048]{2,1,0:T(8,128)(2,1)S(1)} %copy-done.1), kind=kLoop, calls=%fused_computation.3 | loop fusion | flops 2359296 | bytes 3932160 | tf_op jit(solution)/shard_map/convert_element_type | solution.py:408
  118.9 0.0 copy-done
  118.9 1.1 copy.7
Async XLA Ops:
  0.6 115.3 %copy-start.1 = (bf16[12,16,2048]{2,1,0:T(8,128)(2,1)S(1)}, bf16[12,16,2048]{2,1,0:T(8,128)(2,1)}, u32[]{:S(2)}) copy-start(bf16[12,16,2048]{2,1,0:T(8,128)(2,1)} %param.5) | copy-start | bytes 2359300
  115.9 3.0 %copy-start = (f32[12,16,2048]{2,1,0:T(8,128)S(1)}, f32[12,16,2048]{2,1,0:T(8,128)}, u32[]{:S(2)}) copy-start(f32[12,16,2048]{2,1,0:T(8,128)} %get-tuple-element.12) | copy-start | bytes 4718596

commit v2 on v0

v2 whole, which is shorter than its diff:
```python
import functools
import math

import jax
import jax.numpy as jnp
from jax import lax
from jax.experimental import pallas as pl
from jax.experimental.pallas import tpu as pltpu
from jax.sharding import PartitionSpec as P

MESH = pl.DeviceIdType.MESH
F32 = jnp.float32
BF16 = jnp.bfloat16

MATS = 12
BATCHES = 2
MB = MATS // BATCHES
ROWS = 512
COLS = 2048
BAND = 16
SHARDS = 32
ITERS = 5
NA = 4
NB = MB - NA
HB = NB // 2

CHUNKS = 4
WIDTH = COLS // CHUNKS
STEPS = BATCHES * CHUNKS
AHEAD = 2
DONE = 1
EARLY = CHUNKS + 3
NSW = 2048
OUT = 512

linear_term = 3.4445
square_term = -4.775
fourth_term = 2.0315
decay_rate = 0.95
step_size = 0.05
tiny_norm = 1e-07

A_R, A_D, A_S, A_X, B_X, B_R, B_D, B_S = 0, 2, 4, 6, 7, 8, 10, 12
KINDS = 14


def owner_of(k):
    part, j = k // 6, k % 6
    side, i = j // 3, j % 3
    return side * 16 + ((8 * i + 4 * part) // 3) * 2


def owned(me):
    slot = -1
    for k in range(MATS):
        slot = jnp.where(me == owner_of(k), k, slot)
    return slot


def dot(a, b):
    return jnp.dot(a, b, preferred_element_type=F32)


def dot_t(a, b):
    return lax.dot_general(a, b, (((1,), (1,)), ((), ())), preferred_element_type=F32)


def poly_of(gram_ref, poly_ref, scale):
    half = ROWS // 2
    top = gram_ref[:half, :]
    low = gram_ref[half:, half:]
    high_top = top.astype(BF16)
    rest_top = (top - high_top.astype(F32)).astype(BF16)
    high_low = low.astype(BF16)
    rest_low = (low - high_low.astype(F32)).astype(BF16)
    corner = top[:, half:].T
    high_corner = corner.astype(BF16)
    rest_corner = (corner - high_corner.astype(F32)).astype(BF16)
    high_bottom = jnp.concatenate([high_corner, high_low], axis=1)
    rest_bottom = jnp.concatenate([rest_corner, rest_low], axis=1)
    high = jnp.concatenate([high_top, high_bottom], axis=0)
    rest = jnp.concatenate([rest_top, rest_bottom], axis=0)
    cross_top = dot(high_top, rest)
    cross_bottom = dot(high_bottom, rest)
    square_top = dot(high_top, high)
    square_low = dot(high_bottom, high[:, half:])
    flipped = jnp.concatenate([cross_top[:, :half].T, cross_bottom[:, :half].T], axis=1)
    poly_top = square_term * top + fourth_term * (square_top + (cross_top + flipped))
    cross_low = cross_bottom[:, half:]
    poly_low = square_term * low + fourth_term * (square_low + (cross_low + cross_low.T))
    poly_top = scale * poly_top
    poly_ref[:half, :] = poly_top.astype(BF16)
    poly_ref[half:, half:] = (scale * poly_low).astype(BF16)
    poly_ref[half:, :half] = poly_top[:, half:].T.astype(BF16)


def gram_of(block):
    half = ROWS // 2
    return dot_t(block[:half], block), dot_t(block[half:], block[half:])


def set_gram(gram_ref, block):
    half = ROWS // 2
    gram_ref[:half, :], gram_ref[half:, half:] = gram_of(block)


def add_gram(gram_ref, block):
    half = ROWS // 2
    top, low = gram_of(block)
    gram_ref[:half, :] += top
    gram_ref[half:, half:] += low


def begin(gram_ref, scale_ref):
    half = ROWS // 2
    row = lax.broadcasted_iota(jnp.int32, (half, half), 0)
    col = lax.broadcasted_iota(jnp.int32, (half, half), 1)
    diag = jnp.where(row == col, gram_ref[:half, :half] + gram_ref[half:, half:], 0.0)
    total = jnp.sum(jnp.sum(diag, axis=1, keepdims=True), axis=0, keepdims=True)
    scale = 1.0 / (jnp.sqrt(total) + tiny_norm)
    scale_ref[...] = jnp.broadcast_to(scale, scale_ref.shape)
    gram_ref[:half, :] *= scale * scale
    gram_ref[half:, half:] *= scale * scale


def poly_step(gram_ref, poly_ref, scale_ref):
    poly_of(gram_ref, poly_ref, scale_ref[:1, :1])


def apply_columns(matrix, poly_ref, scale_ref, cols, width):
    block = matrix[:, :, cols].reshape(ROWS, width)
    new = (linear_term * scale_ref[:1, :1]) * block.astype(F32) + dot(poly_ref[...], block)
    matrix[:, :, cols] = new.astype(BF16).reshape(SHARDS, BAND, width)


def apply_step(matrix, poly_ref, scale_ref):
    @pl.loop(0, COLS // NSW)
    def _(c):
        apply_columns(matrix, poly_ref, scale_ref, pl.ds(pl.multiple_of(c * NSW, NSW), NSW), NSW)


def gram_step(matrix, gram_ref, scale_ref):
    set_gram(gram_ref, matrix[...].reshape(ROWS, COLS))
    scale_ref[...] = jnp.ones_like(scale_ref)


def kernel(
    grads, momentum_hbm, moment_out, ortho_out,
    momentum,    own_p, own_m, own_c, own_b, a_r, a_d, a_s, a_x, a_send, ax_send,
    b_x, b_u, b_r, b_d, b_s, b_send,
    nest, gathered, gram_ref, poly_ref, scale_ref,
    load_sem, send_sem, recv_sem, gsend_sem, grecv_sem, ssend_sem, srecv_sem, greet_sem,
):
    dp = lax.axis_index("dp")
    me = lax.axis_index("shard")
    y, x = dp // 2, dp % 2
    other = 1 - x
    up_y, down_y, far_y = (y + 1) % 4, (y + 3) % 4, (y + 2) % 4
    up = (up_y * 2 + x, me)
    down = (down_y * 2 + x, me)
    partner = (y * 2 + other, me)
    way = (up, down)
    my_slot = owned(me)
    my_batch = jnp.where(my_slot >= 0, my_slot // MB, -1)

    loads = [
        pltpu.make_async_copy(grads.at[up_y, 0, :, pl.ds(0, NA)], own_p, load_sem.at[0]),
        pltpu.make_async_copy(grads.at[down_y, 1, :, pl.ds(0, NA)], own_m, load_sem.at[1]),
        pltpu.make_async_copy(grads.at[y, :, :, pl.ds(0, NA)], own_c, load_sem.at[2]),
        pltpu.make_async_copy(grads.at[:, x, :, pl.ds(NA, NB)], own_b, load_sem.at[3]),
        pltpu.make_async_copy(momentum_hbm, momentum, load_sem.at[4]),
    ]
    for load in loads:
        load.start()

    side, z, core = me // 16, (me // 2) % 8, me % 2

    def along_z(d):
        return (dp, side * 16 + ((z + d + 8) % 8) * 2 + core)

    def signal(semaphore, device):
        pl.semaphore_signal(semaphore, inc=1, device_id=device, device_id_type=MESH)

    barrier = pltpu.get_barrier_semaphore()
    greeted = [up, down, partner, along_z(1), along_z(-1)]
    greeted += [(dp, (1 - side) * 16 + z * 2 + core), (dp, me + 1 - 2 * core), (dp, (1 - side) * 16 + z * 2 + 1 - core)]
    for device in greeted:
        signal(barrier, device)
    pl.semaphore_wait(barrier, len(greeted))

    def greet(turn):
        if turn == 0:
            for d in (1, -1):
                signal(greet_sem.at[0], along_z(d))
        elif turn == 1:
            pl.semaphore_wait(greet_sem.at[0], 2)
            for d in (2, -2):
                signal(greet_sem.at[1], along_z(d))
        elif turn == 2:
            pl.semaphore_wait(greet_sem.at[1], 2)
            signal(greet_sem.at[2], along_z(4))
        else:
            pl.semaphore_wait(greet_sem.at[2], 1)

    greet(0)
    def columns(q):
        return pl.ds(pl.multiple_of((q % CHUNKS) * WIDTH, WIDTH), WIDTH)

    def message(kind, q, src, dst, device):
        return pltpu.make_async_remote_copy(
            src_ref=src, dst_ref=dst, send_sem=send_sem.at[kind], recv_sem=recv_sem.at[kind, q],
            device_id=device, device_id_type=MESH,
        )

    def a_relay(g, q):
        b, cols = q // CHUNKS, columns(q)
        return message(A_R + g, q, grads.at[far_y, g, b, pl.ds(0, NA), :, cols], a_r.at[g, b, :, :, cols], way[g])

    def a_direct(g, q):
        b, cols = q // CHUNKS, columns(q)
        target = (down_y, up_y)[g]
        return message(
            A_D + g, q, grads.at[target, g, b, pl.ds(0, NA), :, cols], a_d.at[g, b, :, :, cols], way[1 - g]
        )

    def a_sum(g, q):
        b, cols = q // CHUNKS, columns(q)
        return message(A_S + g, q, a_send.at[g, b, :, :, cols], a_s.at[g, b, :, :, cols], way[g])

    def a_cross(q):
        b, cols = q // CHUNKS, columns(q)
        return message(A_X, q, ax_send.at[b, :, :, cols], a_x.at[b, :, :, cols], partner)

    def b_cross(q):
        b, cols = q // CHUNKS, columns(q)
        return message(
            B_X, q, grads.at[:, other, b, pl.ds(NA, NB), :, cols], b_x.at[:, b, :, :, cols], partner
        )

    def b_relay(g, q):
        b, cols = q // CHUNKS, columns(q)
        return message(
            B_R + g, q, b_u.at[far_y, b, pl.ds(g * HB, HB), :, cols], b_r.at[g, b, :, :, cols], way[g]
        )

    def b_direct(g, q):
        b, cols = q // CHUNKS, columns(q)
        target = (down_y, up_y)[g]
        return message(
            B_D + g, q, b_u.at[target, b, pl.ds(g * HB, HB), :, cols], b_d.at[g, b, :, :, cols], way[1 - g]
        )

    def b_sum(g, q):
        b, cols = q // CHUNKS, columns(q)
        return message(B_S + g, q, b_send.at[g, b, :, :, cols], b_s.at[g, b, :, :, cols], way[g])

    def issue(q):
        b_cross(q).start()
        for g in (0, 1):
            a_relay(g, q).start()
        for g in (0, 1):
            a_direct(g, q).start()

    def stage1(q):
        b, cols = q // CHUNKS, columns(q)
        own = (own_p, own_m)
        for g in (0, 1):
            a_relay(g, q).wait_recv()
            total = own[g][b, :, :, cols].astype(F32) + a_r[g, b, :, :, cols].astype(F32)
            a_send[g, b, :, :, cols] = total.astype(BF16)
            a_sum(g, q).start()
        b_cross(q).wait_recv()
        for t in range(4):
            total = own_b[t, b, :, :, cols].astype(F32) + b_x[t, b, :, :, cols].astype(F32)
            b_u[t, b, :, :, cols] = total.astype(BF16)
        for g in (0, 1):
            b_relay(g, q).start()
        for g in (0, 1):
            b_direct(g, q).start()

    def a_total(g, q):
        b, cols = q // CHUNKS, columns(q)
        mine = own_c[g, b, :, :, cols].astype(F32)
        return mine + a_d[g, b, :, :, cols].astype(F32) + a_s[g, b, :, :, cols].astype(F32)

    def stage2(q):
        b, cols = q // CHUNKS, columns(q)
        for g in (0, 1):
            a_direct(g, q).wait_recv()
            a_sum(g, q).wait_recv()
        ax_send[b, :, :, cols] = a_total(other, q).astype(BF16)
        a_cross(q).start()
        own = (up_y, down_y)
        for g in (0, 1):
            b_relay(g, q).wait_recv()
            mine = own_b[own[g], b, g * HB:(g + 1) * HB, :, cols].astype(F32)
            crossed = b_x[own[g], b, g * HB:(g + 1) * HB, :, cols].astype(F32)
            b_send[g, b, :, :, cols] = (mine + crossed + b_r[g, b, :, :, cols].astype(F32)).astype(BF16)
            b_sum(g, q).start()

    def finish(b, first, gradient, cols):
        count = gradient.shape[0]
        moment = decay_rate * momentum[b, first:first + count, :, cols] + gradient
        moment_out[b, first:first + count, :, cols] = moment
        nest[b, first:first + count, :, cols] = (gradient + decay_rate * moment).astype(BF16)

    def stage3(q):
        b, cols = q // CHUNKS, columns(q)
        for g in (0, 1):
            b_direct(g, q).wait_recv()
            b_sum(g, q).wait_recv()
            mine = own_b[y, b, g * HB:(g + 1) * HB, :, cols].astype(F32)
            crossed = b_x[y, b, g * HB:(g + 1) * HB, :, cols].astype(F32)
            arrived = b_d[g, b, :, :, cols].astype(F32) + b_s[g, b, :, :, cols].astype(F32)
            finish(b, NA + g * HB, mine + crossed + arrived, cols)
        a_cross(q).wait_recv()
        finish(b, 0, a_total(x, q) + a_x[b, :, :, cols].astype(F32), cols)

        @pl.loop(0, MB)
        def _(j):
            owner = owner_of(b * MB + j)

            @pl.when(owner == me)
            def _():
                pltpu.make_async_copy(nest.at[b, j, :, cols], gathered.at[me, :, cols], grecv_sem.at[q]).start()

            @pl.when(owner != me)
            def _():
                pltpu.make_async_remote_copy(
                    src_ref=nest.at[b, j, :, cols], dst_ref=gathered.at[me, :, cols],
                    send_sem=gsend_sem.at[b, j], recv_sem=grecv_sem.at[q],
                    device_id=(dp, owner), device_id_type=MESH,
                ).start()

    def arrived(q):
        whole = gathered.at[:, :, columns(q)]
        pltpu.make_async_copy(whole, whole, grecv_sem.at[q]).wait()

    for q in range(AHEAD):
        issue(q)
    gram_ref[...] = jnp.zeros_like(gram_ref)
    for load in loads:
        load.wait()

    def guarded(step, offset, stage):
        @pl.when(jnp.logical_and(step >= offset, step < STEPS + offset))
        def _():
            stage(step - offset)

    @pl.loop(0, STEPS + 2)
    def _(step):
        turn = jnp.logical_and(my_batch == 0, jnp.logical_and(step >= EARLY, step < EARLY + DONE))

        @pl.when(jnp.logical_and(my_batch == 0, step == EARLY))
        def _():
            for q in range(CHUNKS):
                arrived(q)
            set_gram(gram_ref, gathered[...].reshape(ROWS, COLS))
            begin(gram_ref, scale_ref)

        guarded(step, 0, stage1)

        @pl.when(turn)
        def _():
            poly_step(gram_ref, poly_ref, scale_ref)

        for round in (0, 1, 2):
            pl.when(step == round)(functools.partial(greet, round + 1))
        guarded(step, 1, stage2)

        @pl.when(turn)
        def _():
            apply_step(gathered, poly_ref, scale_ref)

        guarded(step, 2, stage3)
        guarded(step, -AHEAD, issue)

        @pl.when(turn)
        def _():
            gram_step(gathered, gram_ref, scale_ref)

    @pl.when(my_batch == 1)
    def _():
        @pl.loop(CHUNKS, STEPS)
        def _(q):
            arrived(q)
            add_gram(gram_ref, gathered[:, :, columns(q)].reshape(ROWS, WIDTH))

        begin(gram_ref, scale_ref)

    @pl.when(my_batch >= 0)
    def _():
        @pl.loop(jnp.where(my_batch == 0, DONE, 0), ITERS - 1)
        def _(it):
            poly_step(gram_ref, poly_ref, scale_ref)
            apply_step(gathered, poly_ref, scale_ref)
            gram_step(gathered, gram_ref, scale_ref)

        poly_step(gram_ref, poly_ref, scale_ref)
        slot_batch, slot_j = my_slot // MB, my_slot % MB

        @pl.loop(0, COLS // OUT)
        def _(c):
            cols = pl.ds(pl.multiple_of(c * OUT, OUT), OUT)
            apply_columns(gathered, poly_ref, scale_ref, cols, OUT)
            target = ortho_out.at[slot_batch, slot_j, :, cols]
            pltpu.make_async_copy(gathered.at[me, :, cols], target, srecv_sem.at[slot_batch, slot_j]).start()

            @pl.loop(1, SHARDS)
            def _(r):
                to = (me + r) % SHARDS
                pltpu.make_async_remote_copy(
                    src_ref=gathered.at[to, :, cols], dst_ref=target,
                    send_sem=ssend_sem.at[c], recv_sem=srecv_sem.at[slot_batch, slot_j],
                    device_id=(dp, to), device_id_type=MESH,
                ).start()

    @pl.loop(0, MATS)
    def _(k):
        b, j = k // MB, k % MB

        @pl.when(owner_of(k) != me)
        def _():
            pltpu.make_async_copy(nest.at[b, j], nest.at[b, j], gsend_sem.at[b, j]).wait()

    def drain(kind, whole):
        pltpu.make_async_copy(whole, whole, send_sem.at[kind]).wait()

    for g in (0, 1):
        for kind in (A_R, A_D, A_S):
            drain(kind + g, a_s.at[g])
        for kind in (B_R, B_D, B_S):
            drain(kind + g, b_s.at[g])
    drain(A_X, a_x)
    drain(B_X, b_x)

    @pl.when(my_batch >= 0)
    def _():
        @pl.loop(0, COLS // OUT)
        def _(c):
            sent = gathered.at[pl.ds(0, SHARDS - 1), :, pl.ds(pl.multiple_of(c * OUT, OUT), OUT)]
            pltpu.make_async_copy(sent, sent, ssend_sem.at[c]).wait()

    @pl.loop(0, MATS)
    def _(k):
        whole = ortho_out.at[k // MB, k % MB]
        pltpu.make_async_copy(whole, whole, srecv_sem.at[k // MB, k % MB]).wait()


def body(grad_parts, momentum, weight):
    vmem = pl.BlockSpec(memory_space=pltpu.VMEM)
    grads = grad_parts.reshape(4, 2, BATCHES, MB, BAND, COLS)
    a_block, b_block = (BATCHES, NA, BAND, COLS), (BATCHES, HB, BAND, COLS)
    x_block = (BATCHES, NB, BAND, COLS)

    def buf(*shape):
        return pltpu.VMEM(shape, BF16)

    moment, ortho = pl.pallas_call(
        kernel,
        out_shape=(
            jax.ShapeDtypeStruct((BATCHES, MB, BAND, COLS), F32),
            jax.ShapeDtypeStruct((BATCHES, MB, BAND, COLS), BF16),
        ),
        in_specs=[pl.BlockSpec(memory_space=pl.ANY)] * 2,
        out_specs=(vmem, vmem),
        scratch_shapes=[
            pltpu.VMEM((BATCHES, MB, BAND, COLS), F32),
            buf(*a_block), buf(*a_block), buf(2, *a_block), buf(4, *x_block),
            buf(2, *a_block), buf(2, *a_block), buf(2, *a_block), buf(*a_block), buf(2, *a_block), buf(*a_block),
            buf(4, *x_block), buf(4, *x_block),
            buf(2, *b_block), buf(2, *b_block), buf(2, *b_block), buf(2, *b_block),
            buf(BATCHES, MB, BAND, COLS),
            buf(SHARDS, BAND, COLS),
            pltpu.VMEM((ROWS, ROWS), F32), pltpu.VMEM((ROWS, ROWS), BF16), pltpu.VMEM((8, 128), F32),
            pltpu.SemaphoreType.DMA((5,)),
            pltpu.SemaphoreType.DMA((KINDS,)), pltpu.SemaphoreType.DMA((KINDS, STEPS)),
            pltpu.SemaphoreType.DMA((BATCHES, MB)), pltpu.SemaphoreType.DMA((STEPS,)),
            pltpu.SemaphoreType.DMA((COLS // OUT,)), pltpu.SemaphoreType.DMA((BATCHES, MB)),
            pltpu.SemaphoreType.REGULAR((3,)),
        ],
        compiler_params=pltpu.CompilerParams(
            collective_id=0, has_side_effects=True, vmem_limit_bytes=56 * 1024 * 1024
        ),
        name="muon_step",
    )(grads, momentum.reshape(BATCHES, MB, BAND, COLS))
    shape_scale = 0.2 * math.sqrt(max(ROWS, COLS))
    scaled = shape_scale * ortho.reshape(MATS, BAND, COLS).astype(F32)
    fresh = (weight.astype(F32) - step_size * scaled).astype(BF16)
    return (moment.reshape(MATS, BAND, COLS), scaled, fresh)


def solution(mesh):
    return jax.shard_map(
        body,
        mesh=mesh,
        in_specs=(P("dp", None, "shard", None), P("dp", "shard", None), P("dp", "shard", None)),
        out_specs=(P("dp", "shard", None), P("dp", "shard", None), P("dp", "shard", None)),
        check_vma=False,
    )
```

time: 491 us -> 111 us (0.23)
  waiting for transfers between devices: 349 us -> 0 us
  Pallas kernels: 0 us -> 105 us
  blocking collectives: 80.4 us -> 0 us
  other arithmetic: 20.2 us -> 3.69 us
  between operations: 15.4 us -> 0.65 us
  starting transfers between devices: 10 us -> 0 us
  local copies, waits for them, and re-layouts: 8.02 us -> 1.74 us
  matrix products: 5.88 us -> 0 us
    reduce_scatter x1 -> x0, waiting for transfers between devices: 255 us -> none  [body(): lax.psum_scatter(grad_parts.astype(jnp.float32), 'dp', scatter_dimension=...]
    pallas_call x0 -> x1, Pallas kernels: none -> 105 us  [body(): pl.pallas_call(kernel, out_shape=(jax.ShapeDtypeStruct((BATCHES, MB, BAND...]
    all_to_all x1 -> x0, waiting for transfers between devices: 94.9 us -> none  [body(): lax.all_to_all(slots, 'shard', split_axis=0, concat_axis=0, tiled=True)]
    all_to_all x1 -> x0, blocking collectives: 80.4 us -> none  [body(): lax.all_to_all(result.reshape(shards, shard_rows, columns), 'shard', spli...]
    convert_element_type x2 -> x1, other arithmetic: 12.8 us -> 1.1 us  [body(): fresh = (weight.astype(F32) - step_size * scaled).astype(BF16)]
    all_to_all x1 -> x0, starting transfers between devices: 9.98 us -> none  [body(): lax.all_to_all(slots, 'shard', split_axis=0, concat_axis=0, tiled=True)]
    dot_general x2 -> x0, matrix products: 5.88 us -> none  [the longest x1 3.3 us: body(): jnp.einsum('sk,src->krc', selector.astype(jnp.bfloat16), returned, prefer...]
  transfers between devices with their start and end apart: 2 -> 0, of which waited for: 2 -> 0; matrix products, arithmetic and copies ran while one was open for 0% -> 0% of each run, Pallas kernels for 0% -> 0%
where the time goes in v2:
time: 111 us
  Pallas kernels  105 us (95%)
  other arithmetic  3.69 us (3%)
  local copies, waits for them, and re-layouts  1.74 us (2%)
    pallas_call x1, Pallas kernels, body(): pl.pallas_call(kernel, out_shape=(jax.ShapeDtypeStruct((BATCHES, MB, BAND...  105 us
    mul x1, other arithmetic, body(): fresh = (weight.astype(F32) - step_size * scaled).astype(BF16)  2.59 us

profile of v2, /device:TPU:1, one launch (start us, length us, event | category | flops | bytes accessed | tf_op | source)
XLA Modules:
  0.0 111.1 jit_solution(10322695567363946979)
XLA Ops:
  0.6 105.0 %muon_step.1 = (f32[2,6,16,2048]{3,2,1,0:T(8,128)}, bf16[2,6,16,2048]{3,2,1,0:T(8,128)(2,1)}) custom-call(bf16[4,2,2,6,16,2048]{5,4,3,2,1,0:T(8,128)(2,1)} %bitcast.8, f32[2,6,16,2048]{3,2,1,0:T(8,128)} %bitcast.11), custom_call_target="tpu_custom_call" | custom-call | tf_op jit(solution)/shard_map/muon_step/pallas_call | solution.py:459
  105.6 0.0 copy-start.1
  105.6 2.6 %convert_multiply_fusion = (f32[2,6,16,2048]{3,2,1,0:T(8,128)S(1)}, f32[2,6,16,2048]{3,2,1,0:T(8,128)}) fusion(bf16[2,6,16,2048]{3,2,1,0:T(8,128)(2,1)} %get-tuple-element.6), kind=kLoop, calls=%fused_computation | loop fusion | flops 1179648 | bytes 3932160 | tf_op jit(solution)/shard_map/mul | solution.py:489
  108.2 0.0 copy-done.1
  108.2 0.0 copy-start
  108.2 1.1 fusion
  109.3 0.6 copy-done
  109.9 1.1 %copy.7 = f32[12,16,2048]{2,1,0:T(8,128)} copy(f32[12,16,2048]{2,1,0:T(8,128)S(1)} %bitcast.9) | data formatting | bytes 3145728
Async XLA Ops:
  105.6 2.6 %copy-start.1 = (bf16[12,16,2048]{2,1,0:T(8,128)(2,1)S(1)}, bf16[12,16,2048]{2,1,0:T(8,128)(2,1)}, u32[]{:S(2)}) copy-start(bf16[12,16,2048]{2,1,0:T(8,128)(2,1)} %param.5) | copy-start | bytes 2359300
  108.2 1.7 %copy-start = (f32[2,6,16,2048]{3,2,1,0:T(8,128)S(1)}, f32[2,6,16,2048]{3,2,1,0:T(8,128)}, u32[]{:S(2)}) copy-start(f32[2,6,16,2048]{3,2,1,0:T(8,128)} %get-tuple-element.5) | copy-start | bytes 4718596

commit v3 on v2

--- a/solution.py
+++ b/solution.py
@@ -31,7 +31,7 @@
 DONE = 1
 EARLY = CHUNKS + 3
 NSW = 2048
-OUT = 512
+OUT = 1024
 
 linear_term = 3.4445
 square_term = -4.775
@@ -145,11 +145,11 @@
 
 
 def kernel(
-    grads, momentum_hbm, moment_out, ortho_out,
-    momentum,    own_p, own_m, own_c, own_b, a_r, a_d, a_s, a_x, a_send, ax_send,
+    grads, momentum_hbm, moment_hbm, ortho_out,
+    momentum, moment_out,    own_p, own_m, own_c, own_b, a_r, a_d, a_s, a_x, a_send, ax_send,
     b_x, b_u, b_r, b_d, b_s, b_send,
     nest, gathered, gram_ref, poly_ref, scale_ref,
-    load_sem, send_sem, recv_sem, gsend_sem, grecv_sem, ssend_sem, srecv_sem, greet_sem,
+    load_sem, send_sem, recv_sem, gsend_sem, grecv_sem, ssend_sem, srecv_sem, greet_sem, moment_sem,
 ):
     dp = lax.axis_index("dp")
     me = lax.axis_index("shard")
@@ -304,6 +304,10 @@
         moment_out[b, first:first + count, :, cols] = moment
         nest[b, first:first + count, :, cols] = (gradient + decay_rate * moment).astype(BF16)
 
+    def moment_store(q):
+        b, cols = q // CHUNKS, columns(q)
+        return pltpu.make_async_copy(moment_out.at[b, :, :, cols], moment_hbm.at[b, :, :, cols], moment_sem.at[q])
+
     def stage3(q):
         b, cols = q // CHUNKS, columns(q)
         for g in (0, 1):
@@ -315,6 +319,7 @@
             finish(b, NA + g * HB, mine + crossed + arrived, cols)
         a_cross(q).wait_recv()
         finish(b, 0, a_total(x, q) + a_x[b, :, :, cols].astype(F32), cols)
+        moment_store(q).start()
 
         @pl.loop(0, MB)
         def _(j):
@@ -423,6 +428,10 @@
         def _():
             pltpu.make_async_copy(nest.at[b, j], nest.at[b, j], gsend_sem.at[b, j]).wait()
 
+    @pl.loop(0, STEPS)
+    def _(q):
+        moment_store(q).wait()
+
     def drain(kind, whole):
         pltpu.make_async_copy(whole, whole, send_sem.at[kind]).wait()
 
@@ -447,8 +456,17 @@
         pltpu.make_async_copy(whole, whole, srecv_sem.at[k // MB, k % MB]).wait()
 
 
+PIECE = 3
+
+
+def outputs(moment, ortho, weight, moment_out, update_out, weight_out):
+    moment_out[...] = moment[...]
+    scaled = (0.2 * math.sqrt(max(ROWS, COLS))) * ortho[...].astype(F32)
+    update_out[...] = scaled
+    weight_out[...] = (weight[...].astype(F32) - step_size * scaled).astype(BF16)
+
+
 def body(grad_parts, momentum, weight):
-    vmem = pl.BlockSpec(memory_space=pltpu.VMEM)
     grads = grad_parts.reshape(4, 2, BATCHES, MB, BAND, COLS)
     a_block, b_block = (BATCHES, NA, BAND, COLS), (BATCHES, HB, BAND, COLS)
     x_block = (BATCHES, NB, BAND, COLS)
@@ -463,9 +481,9 @@
             jax.ShapeDtypeStruct((BATCHES, MB, BAND, COLS), BF16),
         ),
         in_specs=[pl.BlockSpec(memory_space=pl.ANY)] * 2,
-        out_specs=(vmem, vmem),
+        out_specs=(pl.BlockSpec(memory_space=pl.ANY),) * 2,
         scratch_shapes=[
-            pltpu.VMEM((BATCHES, MB, BAND, COLS), F32),
+            pltpu.VMEM((BATCHES, MB, BAND, COLS), F32), pltpu.VMEM((BATCHES, MB, BAND, COLS), F32),
             buf(*a_block), buf(*a_block), buf(2, *a_block), buf(4, *x_block),
             buf(2, *a_block), buf(2, *a_block), buf(2, *a_block), buf(*a_block), buf(2, *a_block), buf(*a_block),
             buf(4, *x_block), buf(4, *x_block),
@@ -477,17 +495,29 @@
             pltpu.SemaphoreType.DMA((KINDS,)), pltpu.SemaphoreType.DMA((KINDS, STEPS)),
             pltpu.SemaphoreType.DMA((BATCHES, MB)), pltpu.SemaphoreType.DMA((STEPS,)),
             pltpu.SemaphoreType.DMA((COLS // OUT,)), pltpu.SemaphoreType.DMA((BATCHES, MB)),
-            pltpu.SemaphoreType.REGULAR((3,)),
+            pltpu.SemaphoreType.REGULAR((3,)), pltpu.SemaphoreType.DMA((STEPS,)),
         ],
         compiler_params=pltpu.CompilerParams(
             collective_id=0, has_side_effects=True, vmem_limit_bytes=56 * 1024 * 1024
         ),
         name="muon_step",
     )(grads, momentum.reshape(BATCHES, MB, BAND, COLS))
-    shape_scale = 0.2 * math.sqrt(max(ROWS, COLS))
-    scaled = shape_scale * ortho.reshape(MATS, BAND, COLS).astype(F32)
-    fresh = (weight.astype(F32) - step_size * scaled).astype(BF16)
-    return (moment.reshape(MATS, BAND, COLS), scaled, fresh)
+    block = pl.BlockSpec((PIECE, BAND, COLS), lambda i: (i, 0, 0))
+    return tuple(
+        pl.pallas_call(
+            outputs,
+            grid=(MATS // PIECE,),
+            out_shape=(
+                jax.ShapeDtypeStruct((MATS, BAND, COLS), F32),
+                jax.ShapeDtypeStruct((MATS, BAND, COLS), F32),
+                jax.ShapeDtypeStruct((MATS, BAND, COLS), BF16),
+            ),
+            in_specs=[block] * 3,
+            out_specs=(block,) * 3,
+            compiler_params=pltpu.CompilerParams(vmem_limit_bytes=56 * 1024 * 1024),
+            name="outputs",
+        )(moment.reshape(MATS, BAND, COLS), ortho.reshape(MATS, BAND, COLS), weight)
+    )
 
 
 def solution(mesh):

time: 111 us -> 108 us (0.973)
  other arithmetic: 3.69 us -> 0 us
  Pallas kernels: 105 us -> 107 us
  local copies, waits for them, and re-layouts: 1.74 us -> 0 us
    pallas_call x0 -> x1, Pallas kernels: none -> 4.36 us  [body(): pl.pallas_call(outputs, grid=(MATS // PIECE,), out_shape=(jax.ShapeDtypeS...]
    mul x1 -> x0, other arithmetic: 2.59 us -> none  [body(): fresh = (weight.astype(F32) - step_size * scaled).astype(BF16)]
    pallas_call x1, Pallas kernels: 105 us -> 103 us  [body(): pl.pallas_call(kernel, out_shape=(jax.ShapeDtypeStruct((BATCHES, MB, BAND...]
    unnamed x5 -> x0, local copies, waits for them, and re-layouts: 1.74 us -> none
where the time goes in v3:
time: 108 us
  Pallas kernels  107 us (99%)
    pallas_call x1, Pallas kernels, body(): pl.pallas_call(kernel, out_shape=(jax.ShapeDtypeStruct((BATCHES, MB, BAND...  103 us
    pallas_call x1, Pallas kernels, body(): pl.pallas_call(outputs, grid=(MATS // PIECE,), out_shape=(jax.ShapeDtypeS...  4.36 us

profile of v3, /device:TPU:1, one launch (start us, length us, event | category | flops | bytes accessed | tf_op | source)
XLA Modules:
  0.0 107.8 jit_solution(5520578686251919460)
XLA Ops:
  0.6 102.8 %muon_step.1 = (f32[2,6,16,2048]{3,2,1,0:T(8,128)}, bf16[2,6,16,2048]{3,2,1,0:T(8,128)(2,1)}) custom-call(bf16[4,2,2,6,16,2048]{5,4,3,2,1,0:T(8,128)(2,1)} %bitcast.4, f32[2,6,16,2048]{3,2,1,0:T(8,128)} %bitcast.6), custom_call_target="tpu_custom_call" | custom-call | tf_op jit(solution)/shard_map/muon_step/pallas_call | solution.py:477
  103.5 4.4 %outputs.1 = (f32[12,16,2048]{2,1,0:T(8,128)}, f32[12,16,2048]{2,1,0:T(8,128)}, bf16[12,16,2048]{2,1,0:T(8,128)(2,1)}) custom-call(f32[12,16,2048]{2,1,0:T(8,128)} %bitcast.5, bf16[12,16,2048]{2,1,0:T(8,128)(2,1)} %bitcast.7, bf16[12,16,2048]{2,1,0:T(8,128)(2,1)} %weight.1), custom_call_target="tpu_custom_call" | custom-call | tf_op jit(solution)/shard_map/outputs/pallas_call | solution.py:507

commit v4 on v3

--- a/solution.py
+++ b/solution.py
@@ -31,7 +31,7 @@
 DONE = 1
 EARLY = CHUNKS + 3
 NSW = 2048
-OUT = 1024
+OUT = 2048
 
 linear_term = 3.4445
 square_term = -4.775
@@ -308,20 +308,10 @@
         b, cols = q // CHUNKS, columns(q)
         return pltpu.make_async_copy(moment_out.at[b, :, :, cols], moment_hbm.at[b, :, :, cols], moment_sem.at[q])
 
-    def stage3(q):
-        b, cols = q // CHUNKS, columns(q)
-        for g in (0, 1):
-            b_direct(g, q).wait_recv()
-            b_sum(g, q).wait_recv()
-            mine = own_b[y, b, g * HB:(g + 1) * HB, :, cols].astype(F32)
-            crossed = b_x[y, b, g * HB:(g + 1) * HB, :, cols].astype(F32)
-            arrived = b_d[g, b, :, :, cols].astype(F32) + b_s[g, b, :, :, cols].astype(F32)
-            finish(b, NA + g * HB, mine + crossed + arrived, cols)
-        a_cross(q).wait_recv()
-        finish(b, 0, a_total(x, q) + a_x[b, :, :, cols].astype(F32), cols)
-        moment_store(q).start()
-
-        @pl.loop(0, MB)
+    def to_owners(q, first, last):
+        b, cols = q // CHUNKS, columns(q)
+
+        @pl.loop(first, last)
         def _(j):
             owner = owner_of(b * MB + j)
 
@@ -336,6 +326,22 @@
                     send_sem=gsend_sem.at[b, j], recv_sem=grecv_sem.at[q],
                     device_id=(dp, owner), device_id_type=MESH,
                 ).start()
+
+    def stage3(q):
+        b, cols = q // CHUNKS, columns(q)
+        for g in (0, 1):
+            b_direct(g, q).wait_recv()
+            b_sum(g, q).wait_recv()
+            mine = own_b[y, b, g * HB:(g + 1) * HB, :, cols].astype(F32)
+            crossed = b_x[y, b, g * HB:(g + 1) * HB, :, cols].astype(F32)
+            arrived = b_d[g, b, :, :, cols].astype(F32) + b_s[g, b, :, :, cols].astype(F32)
+            finish(b, NA + g * HB, mine + crossed + arrived, cols)
+        to_owners(q, NA, MB)
+        a_cross(q).wait_recv()
+        finish(b, 0, a_total(x, q) + a_x[b, :, :, cols].astype(F32), cols)
+        moment_store(q).start()
+
+        to_owners(q, 0, NA)
 
     def arrived(q):
         whole = gathered.at[:, :, columns(q)]
@@ -456,7 +462,7 @@
         pltpu.make_async_copy(whole, whole, srecv_sem.at[k // MB, k % MB]).wait()
 
 
-PIECE = 3
+PIECE = 4
 
 
 def outputs(moment, ortho, weight, moment_out, update_out, weight_out):

time: 108 us -> 108 us (level)
  no operation moved by 1% of the time
where the time goes in v4:
time: 108 us
  Pallas kernels  107 us (99%)
    pallas_call x1, Pallas kernels, body(): pl.pallas_call(kernel, out_shape=(jax.ShapeDtypeStruct((BATCHES, MB, BAND...  102 us
    pallas_call x1, Pallas kernels, body(): pl.pallas_call(outputs, grid=(MATS // PIECE,), out_shape=(jax.ShapeDtypeS...  4.53 us

profile of v4, /device:TPU:1, one launch (start us, length us, event | category | flops | bytes accessed | tf_op | source)
XLA Modules:
  0.0 107.6 jit_solution(11580499140139520265)
XLA Ops:
  0.6 102.5 %muon_step.1 = (f32[2,6,16,2048]{3,2,1,0:T(8,128)}, bf16[2,6,16,2048]{3,2,1,0:T(8,128)(2,1)}) custom-call(bf16[4,2,2,6,16,2048]{5,4,3,2,1,0:T(8,128)(2,1)} %bitcast.4, f32[2,6,16,2048]{3,2,1,0:T(8,128)} %bitcast.6), custom_call_target="tpu_custom_call" | custom-call | tf_op jit(solution)/shard_map/muon_step/pallas_call | solution.py:483
  103.1 4.5 %outputs.1 = (f32[12,16,2048]{2,1,0:T(8,128)}, f32[12,16,2048]{2,1,0:T(8,128)}, bf16[12,16,2048]{2,1,0:T(8,128)(2,1)}) custom-call(f32[12,16,2048]{2,1,0:T(8,128)} %bitcast.5, bf16[12,16,2048]{2,1,0:T(8,128)(2,1)} %bitcast.7, bf16[12,16,2048]{2,1,0:T(8,128)(2,1)} %weight.1), custom_call_target="tpu_custom_call" | custom-call | tf_op jit(solution)/shard_map/outputs/pallas_call | solution.py:513
